TPU v7x, 32 devices: a whole 2x2x4 slice. The times are simulated.
32 devices in a mesh: grp: 4 (over y, x), sub: 8 (over z, core).
Axes of the slice: x: 2, y: 2, z: 4, core: 2. Of those that a mesh axis runs over, the one named last changes fastest.
Arguments:
- solution: float32 [4, 8, 16, 512], P('grp', 'sub'), may hold values from -6 to 6
- residual: float32 [4, 8, 16, 512], P('grp', 'sub'), as said below
- direction: float32 [4, 8, 16, 512], P('grp', 'sub'), as said below
- inner_old: float32 [16], replicated, may hold values from 0.5 to 2
- interior: bfloat16 [4, 8, 16, 1536], P('grp', 'sub'), may hold values from -6 to 6
- weights: float32 [4, 8, 512], P('grp', 'sub'), as said below
- neighbours: int32 [4, 8, 4], P('grp', 'sub'), may hold values from -1 to 7, as said below
- coarse_rows: int32 [4, 8, 12], P('grp', 'sub'), may hold values from -1 to 119, as said below
- coarse_basis_matrix: float32 [4, 8, 12, 512], P('grp', 'sub'), may hold values from -0.5 to 0.5
- local_solver: bfloat16 [4, 8, 512, 512], P('grp', 'sub'), as said below
- schur_matrix: bfloat16 [4, 8, 512, 512], P('grp', 'sub'), as said below
- extension_values: bfloat16 [4, 8, 12, 2, 128, 128], P('grp', 'sub'), may hold values from -0.375 to 0.375
- extension_block_index: int32 [4, 8, 12, 2], P('grp', 'sub'), may hold values from 0 to 3
- coarse_inverse: float32 [120, 120], P('sub'), as said below
Outputs:
- solution_new: float32 [4, 8, 16, 512], P('grp', 'sub')
- residual_new: float32 [4, 8, 16, 512], P('grp', 'sub')
- direction_new: float32 [4, 8, 16, 512], P('grp', 'sub')
- interior_new: bfloat16 [4, 8, 16, 1536], P('grp', 'sub')
- inner_new: float32 [16], replicated
Inputs may be any that keep to these rules, and one draw needn't show every extreme that they name: Within a group the relation is symmetric: if neighbours[g, s, k] = t >= 0 then neighbours[g, t, k XOR 1] = s; the neighbours of one subdomain are distinct; -1 marks an absent block. `coarse_rows`: both subdomains of a shared face block list the same 3 rows for it, each coarse row is named by exactly two entries, and absent blocks hold -1. On a shared face the two sides' weights add up to 1; absent blocks hold 0. `residual`: equal on the two sides of every shared face, 0 on absent blocks. `direction`: equal on the two sides of every shared face, 0 on absent blocks. `local_solver`: Symmetric, with a positive diagonal larger than the sum of the magnitudes of its row's other entries. `schur_matrix`: Symmetric, with a positive diagonal larger than the sum of the magnitudes of its row's other entries. `coarse_inverse`: symmetric positive definite.
All inputs are finite; a program needn't handle non-finite values.
Results may differ from a plain program's by a relative error of at most 0.0019.
The roundings to bfloat16 on the way count: a program that leaves them out, or rounds other values in their place, can miss the bound.
Values sent between devices are 32-bit elements; how exact they have to be, the bound alone decides.
A program may use at most 64 MiB of HBM per device.

v0:
```python
import jax
import jax.numpy as jnp
from jax import lax
from jax.sharding import PartitionSpec as P

PRECISE = lax.Precision.HIGHEST


def contract(former, latter, former_dim, latter_dim):
    return lax.dot_general(
        former, latter, (((former_dim,), (latter_dim,)), ((), ())), precision=PRECISE
    )


def outgoing(blocks, neighbour, peer_count):
    active = (neighbour >= 0).astype(jnp.float32)
    clipped = jnp.maximum(neighbour, 0)
    outbound = jnp.transpose(blocks * active[None, :, None], (1, 0, 2))
    buffer = jnp.zeros((peer_count, blocks.shape[0], blocks.shape[2]), jnp.float32)
    return buffer.at[clipped].add(outbound)


def incoming(received, neighbour):
    active = (neighbour >= 0).astype(jnp.float32)
    picked = jnp.take(received, jnp.maximum(neighbour, 0), axis=0)
    return jnp.transpose(picked, (1, 0, 2)) * active[None, :, None]


def per_device(
    solution,
    residual,
    direction,
    inner_old,
    interior,
    weights,
    neighbours,
    coarse_rows,
    coarse_basis_matrix,
    local_solver,
    schur_matrix,
    extension_values,
    extension_block_index,
    coarse_inverse,
):
    peer_count = lax.axis_size("sub")
    rhs_count = residual.shape[2]
    local_faces = residual.shape[3]
    neighbour = neighbours[0, 0]
    slot_count = neighbour.shape[0]
    block_size = local_faces // slot_count
    active = jnp.repeat((neighbour >= 0).astype(jnp.float32), block_size)
    current = residual[0, 0]
    weight = weights[0, 0]
    basis_rows = coarse_basis_matrix[0, 0]
    primal = coarse_rows[0, 0]
    coarse_count = coarse_inverse.shape[1]
    face_total = coarse_count // (primal.shape[0] // slot_count) * block_size
    scaled = weight[None, :] * current
    local_solve = jnp.dot(
        scaled.astype(jnp.bfloat16), local_solver[0, 0], preferred_element_type=jnp.float32
    )
    coarse_part = contract(scaled, basis_rows, 1, 1)
    columns = lax.broadcasted_iota(jnp.int32, (primal.shape[0], coarse_count), 1)
    selector = (primal[:, None] == columns).astype(jnp.float32)
    partial_sum = jnp.dot(coarse_part, selector, precision=PRECISE)
    coarse_total = lax.psum(partial_sum, ("grp", "sub"))
    own_solution = contract(coarse_inverse, coarse_total, 1, 1)
    coarse_solution = lax.all_gather(own_solution, "sub", axis=0, tiled=True)
    coarse_local = jnp.dot(selector, coarse_solution, precision=PRECISE)
    correction = contract(coarse_local, basis_rows, 0, 0)
    weighted = weight[None, :] * (local_solve + correction)
    blocks_out = weighted.reshape(rhs_count, slot_count, block_size)
    received = lax.all_to_all(
        outgoing(blocks_out, neighbour, peer_count), "sub", split_axis=0, concat_axis=0, tiled=True
    )
    precond = weighted + incoming(received, neighbour).reshape(rhs_count, local_faces)
    inner_now = lax.psum(jnp.sum(current * precond, axis=1), ("grp", "sub")) / (2.0 * face_total)
    direction_new = precond + (inner_now / inner_old)[:, None] * direction[0, 0]
    direction_half = direction_new.astype(jnp.bfloat16)
    local_image = jnp.dot(direction_half, schur_matrix[0, 0], preferred_element_type=jnp.float32)
    image_blocks = local_image.reshape(rhs_count, slot_count, block_size)
    received_image = lax.all_to_all(
        outgoing(image_blocks, neighbour, peer_count),
        "sub",
        split_axis=0,
        concat_axis=0,
        tiled=True,
    )
    image_sum = active[None, :] * (
        local_image + incoming(received_image, neighbour).reshape(rhs_count, local_faces)
    )
    curve_term = 0.5 * jnp.sum(direction_new * image_sum, axis=1)
    curvature = lax.psum(curve_term, ("grp", "sub")) / face_total
    step_size = inner_now / curvature
    solution_new = solution[0, 0] + step_size[:, None] * direction_new
    residual_new = current - step_size[:, None] * image_sum
    direction_blocks = direction_half.reshape(rhs_count, slot_count, block_size)
    picked = jnp.take(direction_blocks, extension_block_index[0, 0], axis=1)
    extended = jnp.einsum(
        "rbjk,bjkl->rbl", picked, extension_values[0, 0], preferred_element_type=jnp.float32
    )
    extended = extended.reshape(rhs_count, -1)
    interior_new = (interior[0, 0].astype(jnp.float32) + step_size[:, None] * extended).astype(
        jnp.bfloat16
    )
    return (
        solution_new[None, None],
        residual_new[None, None],
        direction_new[None, None],
        interior_new[None, None],
        inner_now,
    )


def solution(mesh):
    in_specs = (
        P("grp", "sub", None, None),
        P("grp", "sub", None, None),
        P("grp", "sub", None, None),
        P(),
        P("grp", "sub", None, None),
        P("grp", "sub", None),
        P("grp", "sub", None),
        P("grp", "sub", None),
        P("grp", "sub", None, None),
        P("grp", "sub", None, None),
        P("grp", "sub", None, None),
        P("grp", "sub", None, None, None, None),
        P("grp", "sub", None, None),
        P("sub", None),
    )
    out_specs = (
        P("grp", "sub", None, None),
        P("grp", "sub", None, None),
        P("grp", "sub", None, None),
        P("grp", "sub", None, None),
        P(),
    )
    return jax.shard_map(
        per_device, mesh=mesh, in_specs=in_specs, out_specs=out_specs, check_vma=False
    )
```

profile of v0, /device:TPU:0, one launch (start us, length us, event | category | flops | bytes accessed | tf_op | source)
XLA Modules:
  0.0 169.0 jit_solution(9950449269539070436)
XLA Ops:
  0.6 0.0 copy-start
  0.6 0.0 copy-start.14
  0.7 0.7 fusion.35
  1.4 0.0 copy-done.14
  1.4 0.0 copy-start.8
  1.4 0.7 copy-done.8
  2.1 0.9 fusion.14
  3.0 0.0 copy-start.11
  3.0 0.7 copy-done.11
  3.7 0.0 copy-start.9
  3.7 0.2 fusion.32
  3.9 0.0 copy-start.1
  3.9 42.0 %psum.21 = f32[16,120]{1,0:T(8,128)S(1)} all-reduce(f32[16,120]{1,0:T(8,128)S(1)} %fusion.32), channel_id=1, replica_groups=mesh['grp'=4,'sub'=8] {'grp','sub'}, use_global_device_ids=true, to_apply=%region_0.0 | all-reduce | flops 1920 | bytes 15360 | tf_op jit(solution)/shard_map/psum | solution.py:66
  45.9 0.0 copy-done.9
  45.9 0.1 convolution_bitcast_fusion.1
  46.0 0.1 copy.35
  46.1 0.0 copy-done.1
  46.1 1.2 fusion.4
  47.3 0.0 copy-start.4
  47.3 14.1 %all-gather = f32[8,15,16]{2,1,0:T(8,128)S(1)} all-gather(f32[1,15,16]{2,1,0:T(8,128)S(1)} %copy.35), channel_id=1, replica_groups=mesh['grp'=4,'sub'=8] {'sub'}, dimensions={0}, use_global_device_ids=true | all-gather | bytes 8640 | tf_op jit(solution)/shard_map/all_gather | solution.py:68
  61.4 0.0 copy-start.3
  61.4 0.2 fusion.31
  61.6 0.0 copy-done.4
  61.6 0.3 fusion
  61.9 0.1 fusion.12
  62.0 0.6 broadcast.107.clone
  62.6 2.0 %scatter_fusion = f32[8,16,128]{2,1,0:T(8,128)} fusion(f32[8,16,128]{2,1,0:T(8,128)} %broadcast.107.clone, s32[4]{0:T(128)S(1)} %maximum_bitcast_fusion, f32[4,16,128]{2,1,0:T(8,128)S(1)} %fusion.12), kind=kCustom, calls=%fused_computation.3 | custom fusion | flops 8192 | bytes 98320 | tf_op jit(solution)/shard_map/scatter-add | solution.py:20
  64.5 0.0 copy-start.10
  64.5 3.6 %all-to-all-start = ((f32[8,16,128]{2,1,0:T(8,128)}), f32[8,16,128]{2,1,0:T(8,128)S(1)}, u32[]{:S(2)}, u32[]{:S(2)}) async-start(f32[8,16,128]{2,1,0:T(8,128)} %scatter_fusion), calls=%async_computation | async-start | bytes 131072 | tf_op jit(solution)/shard_map/all_to_all | solution.py:73
  68.1 0.0 copy-done.10
  68.2 0.1 broadcast_bitcast_fusion
  68.3 0.1 copy.42
  68.4 0.1 reshape.161
  68.5 5.6 %all-to-all-done = f32[8,16,128]{2,1,0:T(8,128)S(1)} async-done(((f32[8,16,128]{2,1,0:T(8,128)}), f32[8,16,128]{2,1,0:T(8,128)S(1)}, u32[]{:S(2)}, u32[]{:S(2)}) %all-to-all-start) | async-done | bytes 65568 | tf_op jit(solution)/shard_map/all_to_all | solution.py:73
  74.1 0.5 gather_fusion.1
  74.6 0.0 copy-start.7
  74.6 0.2 fusion.20
  74.8 0.1 copy.41
  74.9 39.3 %psum.22 = f32[16]{0:T(128)S(1)} all-reduce(f32[16]{0:T(128)S(1)} %fusion.20), channel_id=1, replica_groups=mesh['grp'=4,'sub'=8] {'grp','sub'}, use_global_device_ids=true, to_apply=%region_3.5 | all-reduce | flops 16 | bytes 128 | tf_op jit(solution)/shard_map/psum | solution.py:77
  114.2 0.0 copy-done.12
  114.2 0.0 copy-done.7
  114.2 0.1 convert_bitcast_fusion
  114.3 0.0 copy-start.2
  114.4 0.0 copy-done.3
  114.4 0.2 fusion.2
  114.5 0.1 fusion.11
  114.6 0.6 broadcast.107
  115.2 2.0 %scatter_fusion.1 = f32[8,16,128]{2,1,0:T(8,128)} fusion(f32[8,16,128]{2,1,0:T(8,128)} %broadcast.107, s32[4]{0:T(128)S(1)} %maximum_bitcast_fusion, f32[4,16,128]{2,1,0:T(8,128)S(1)} %fusion.11), kind=kCustom, calls=%fused_computation.4 | custom fusion | flops 8192 | bytes 98320 | tf_op jit(solution)/shard_map/scatter-add | solution.py:20
  117.2 3.3 %all-to-all-start.1 = ((f32[8,16,128]{2,1,0:T(8,128)}), f32[8,16,128]{2,1,0:T(8,128)S(1)}, u32[]{:S(2)}, u32[]{:S(2)}) async-start(f32[8,16,128]{2,1,0:T(8,128)} %scatter_fusion.1), calls=%async_computation.1 | async-start | bytes 131072 | tf_op jit(solution)/shard_map/all_to_all | solution.py:82
  120.6 0.6 gather_fusion
  121.1 0.0 copy-done
  121.1 0.3 convolution_bitcast_fusion
  121.5 4.9 %all-to-all-done.1 = f32[8,16,128]{2,1,0:T(8,128)S(1)} async-done(((f32[8,16,128]{2,1,0:T(8,128)}), f32[8,16,128]{2,1,0:T(8,128)S(1)}, u32[]{:S(2)}, u32[]{:S(2)}) %all-to-all-start.1) | async-done | bytes 65568 | tf_op jit(solution)/shard_map/all_to_all | solution.py:82
  126.4 0.5 gather_fusion.2
  127.0 0.2 multiply_reduce_fusion
  127.2 0.0 copy-start.6
  127.2 40.2 %psum.23 = f32[16]{0:T(128)S(1)} all-reduce(f32[16]{0:T(128)S(1)} %broadcast_multiply_fusion), channel_id=1, replica_groups=mesh['grp'=4,'sub'=8] {'grp','sub'}, use_global_device_ids=true, to_apply=%region_6.8 | all-reduce | flops 16 | bytes 128 | tf_op jit(solution)/shard_map/psum | solution.py:93
  167.4 0.0 copy-done.13
  167.4 0.0 copy-done.2
  167.4 0.0 copy-done.6
  167.5 0.0 copy-start.5
  167.5 0.7 fusion.21
  168.2 0.1 copy-done.5
  168.3 0.7 add_convert_fusion
  (15 shorter events, 0.1 us)
Async XLA Ops:
  0.6 120.5 %copy-start = (bf16[1,1,12,2,128,128]{5,4,3,2,1,0:T(8,128)(2,1)S(1)}, bf16[1,1,12,2,128,128]{5,4,3,2,1,0:T(8,128)(2,1)}, u32[]{:S(2)}) copy-start(bf16[1,1,12,2,128,128]{5,4,3,2,1,0:T(8,128)(2,1)} %param.27) | copy-start | bytes 2359300
  0.6 0.7 copy-start.14
  1.4 0.7 copy-start.8
  3.0 0.7 copy-start.11
  3.7 42.2 %copy-start.9 = (f32[15,120]{1,0:T(8,128)S(1)}, f32[15,120]{1,0:T(8,128)}, u32[]{:S(2)}) copy-start(f32[15,120]{1,0:T(8,128)} %param.29) | copy-start | bytes 21604
  3.9 42.3 %copy-start.1 = (f32[1,1,16,512]{3,2,1,0:T(8,128)S(1)}, f32[1,1,16,512]{3,2,1,0:T(8,128)}, u32[]{:S(2)}) copy-start(f32[1,1,16,512]{3,2,1,0:T(8,128)} %param.17) | copy-start | bytes 98308
  47.3 14.3 %copy-start.4 = (f32[1,1,12,512]{3,1,2,0:T(1,128)S(1)}, f32[1,1,12,512]{3,1,2,0:T(1,128)}, u32[]{:S(2)}) copy-start(f32[1,1,12,512]{3,1,2,0:T(1,128)} %param.24) | copy-start | bytes 73732
  61.4 52.9 %copy-start.3 = (bf16[1,1,512,512]{3,2,1,0:T(8,128)(2,1)S(1)}, bf16[1,1,512,512]{3,2,1,0:T(8,128)(2,1)}, u32[]{:S(2)}) copy-start(bf16[1,1,512,512]{3,2,1,0:T(8,128)(2,1)} %param.26) | copy-start | bytes 1572868
  64.5 3.6 %copy-start.10 = (s32[1,1,12,2]{2,3,1,0:T(2,128)S(1)}, s32[1,1,12,2]{2,3,1,0:T(2,128)}, u32[]{:S(2)}) copy-start(s32[1,1,12,2]{2,3,1,0:T(2,128)} %param.28) | copy-start | bytes 292
  64.5 9.5 %all-to-all-start = ((f32[8,16,128]{2,1,0:T(8,128)}), f32[8,16,128]{2,1,0:T(8,128)S(1)}, u32[]{:S(2)}, u32[]{:S(2)}) async-start(f32[8,16,128]{2,1,0:T(8,128)} %scatter_fusion), calls=%async_computation | async-start | bytes 131072 | tf_op jit(solution)/shard_map/all_to_all | solution.py:73
  74.6 39.6 %copy-start.7 = (f32[1,1,16,512]{3,2,1,0:T(8,128)S(1)}, f32[1,1,16,512]{3,2,1,0:T(8,128)}, u32[]{:S(2)}) copy-start(f32[1,1,16,512]{3,2,1,0:T(8,128)} %param.18) | copy-start | bytes 98308
  74.9 39.3 %copy-start.12 = (f32[16]{0:T(128)S(1)}, f32[16]{0:T(128)}, u32[]{:S(2)}) copy-start(f32[16]{0:T(128)} %param.19) | copy-start | bytes 196
  114.2 53.2 %copy-start.13 = (f32[16]{0:T(128)}, f32[16]{0:T(128)S(1)}, u32[]{:S(2)}) copy-start(f32[16]{0:T(128)S(1)} %get-tuple-element.9) | copy-start | bytes 196
  114.3 53.1 %copy-start.2 = (f32[16,512]{1,0:T(8,128)}, f32[16,512]{1,0:T(8,128)S(1)}, u32[]{:S(2)}) copy-start(f32[16,512]{1,0:T(8,128)S(1)} %get-tuple-element.7) | copy-start | bytes 98308
  117.2 9.2 %all-to-all-start.1 = ((f32[8,16,128]{2,1,0:T(8,128)}), f32[8,16,128]{2,1,0:T(8,128)S(1)}, u32[]{:S(2)}, u32[]{:S(2)}) async-start(f32[8,16,128]{2,1,0:T(8,128)} %scatter_fusion.1), calls=%async_computation.1 | async-start | bytes 131072 | tf_op jit(solution)/shard_map/all_to_all | solution.py:82
  127.2 40.3 %copy-start.6 = (f32[1,1,16,512]{3,2,1,0:T(8,128)S(1)}, f32[1,1,16,512]{3,2,1,0:T(8,128)}, u32[]{:S(2)}) copy-start(f32[1,1,16,512]{3,2,1,0:T(8,128)} %param.16) | copy-start | bytes 98308
  167.5 0.8 copy-start.5
where the time goes:
time: 170 us; the launch traced here: 169 us
  blocking collectives  136 us (80%)
  waiting for transfers between devices  10.5 us (6%)
  starting transfers between devices  6.94 us (4%)
  other arithmetic  6.72 us (4%)
  local copies, waits for them, and re-layouts  4.93 us (3%)
  matrix products  3.31 us (2%)
    psum x1, blocking collectives, per_device(): coarse_total = lax.psum(partial_sum, ('grp', 'sub'))  42 us
    psum x1, blocking collectives, per_device(): curvature = lax.psum(curve_term, ('grp', 'sub')) / face_total  40.2 us
    psum x1, blocking collectives, per_device(): lax.psum(jnp.sum(current * precond, axis=1), ('grp', 'sub'))  39.3 us
    all_gather x1, blocking collectives, per_device(): coarse_solution = lax.all_gather(own_solution, 'sub', axis=0, tiled=True)  14.1 us
    all_to_all x1, waiting for transfers between devices, per_device(): lax.all_to_all(outgoing(blocks_out, neighbour, peer_count), 'sub', split_...  5.6 us
    all_to_all x1, waiting for transfers between devices, per_device(): lax.all_to_all(outgoing(image_blocks, neighbour, peer_count), 'sub', spli...  4.94 us
    scatter-add x2, other arithmetic, outgoing(): return buffer.at[clipped].add(outbound)  3.91 us
    all_to_all x1, starting transfers between devices, per_device(): lax.all_to_all(outgoing(blocks_out, neighbour, peer_count), 'sub', split_...  3.59 us
  transfers between devices with their start and end apart: 2, of which 2 were waited for; matrix products, arithmetic and copies ran while one was open for 1% of the time, Pallas kernels for 0%

commit v1 on v0

--- a/solution.py
+++ b/solution.py
@@ -90,7 +90,7 @@
         local_image + incoming(received_image, neighbour).reshape(rhs_count, local_faces)
     )
     curve_term = 0.5 * jnp.sum(direction_new * image_sum, axis=1)
-    curvature = lax.psum(curve_term, ("grp", "sub")) / face_total
+    curvature = lax.psum(lax.psum(curve_term, "sub"), "grp") / face_total
     step_size = inner_now / curvature
     solution_new = solution[0, 0] + step_size[:, None] * direction_new
     residual_new = current - step_size[:, None] * image_sum

time: 170 us -> 154 us (0.906)
  blocking collectives: 136 us -> 120 us
    psum x1 -> x2, blocking collectives: 40.2 us -> 24.5 us  [per_device(): curvature = lax.psum(lax.psum(curve_term, 'sub'), 'grp') / face_total]
where the time goes in v1:
time: 154 us; the launch traced here: 153 us
  blocking collectives  120 us (78%)
  waiting for transfers between devices  10.5 us (7%)
  starting transfers between devices  6.93 us (4%)
  other arithmetic  6.74 us (4%)
  local copies, waits for them, and re-layouts  4.94 us (3%)
  matrix products  3.31 us (2%)
    psum x1, blocking collectives, per_device(): coarse_total = lax.psum(partial_sum, ('grp', 'sub'))  42 us
    psum x1, blocking collectives, per_device(): lax.psum(jnp.sum(current * precond, axis=1), ('grp', 'sub'))  39.3 us
    psum x2, blocking collectives, per_device(): curvature = lax.psum(lax.psum(curve_term, 'sub'), 'grp') / face_total  24.5 us
    all_gather x1, blocking collectives, per_device(): coarse_solution = lax.all_gather(own_solution, 'sub', axis=0, tiled=True)  14.1 us
    all_to_all x1, waiting for transfers between devices, per_device(): lax.all_to_all(outgoing(blocks_out, neighbour, peer_count), 'sub', split_...  5.6 us
    all_to_all x1, waiting for transfers between devices, per_device(): lax.all_to_all(outgoing(image_blocks, neighbour, peer_count), 'sub', spli...  4.94 us
    scatter-add x2, other arithmetic, outgoing(): return buffer.at[clipped].add(outbound)  3.92 us
    all_to_all x1, starting transfers between devices, per_device(): lax.all_to_all(outgoing(blocks_out, neighbour, peer_count), 'sub', split_...  3.58 us
  transfers between devices with their start and end apart: 2, of which 2 were waited for; matrix products, arithmetic and copies ran while one was open for 1% of the time, Pallas kernels for 0%

profile of v1, /device:TPU:0, one launch (start us, length us, event | category | flops | bytes accessed | tf_op | source)
XLA Modules:
  0.0 153.2 jit_solution(13872363356411360387)
XLA Ops:
  0.6 0.0 copy-start
  0.6 0.0 copy-start.14
  0.7 0.7 fusion.35
  1.4 0.0 copy-done.14
  1.4 0.0 copy-start.8
  1.4 0.7 copy-done.8
  2.1 0.9 fusion.14
  3.0 0.0 copy-start.11
  3.0 0.7 copy-done.11
  3.7 0.0 copy-start.9
  3.7 0.2 fusion.32
  3.9 0.0 copy-start.1
  3.9 42.0 %psum.28 = f32[16,120]{1,0:T(8,128)S(1)} all-reduce(f32[16,120]{1,0:T(8,128)S(1)} %fusion.32), channel_id=1, replica_groups=mesh['grp'=4,'sub'=8] {'grp','sub'}, use_global_device_ids=true, to_apply=%region_0.0 | all-reduce | flops 1920 | bytes 15360 | tf_op jit(solution)/shard_map/psum | solution.py:66
  45.9 0.0 copy-done.9
  45.9 0.1 convolution_bitcast_fusion.1
  46.0 0.1 copy.35
  46.1 0.0 copy-done.1
  46.1 1.2 fusion.4
  47.3 0.0 copy-start.4
  47.3 14.1 %all-gather = f32[8,15,16]{2,1,0:T(8,128)S(1)} all-gather(f32[1,15,16]{2,1,0:T(8,128)S(1)} %copy.35), channel_id=1, replica_groups=mesh['grp'=4,'sub'=8] {'sub'}, dimensions={0}, use_global_device_ids=true | all-gather | bytes 8640 | tf_op jit(solution)/shard_map/all_gather | solution.py:68
  61.4 0.0 copy-start.3
  61.4 0.2 fusion.31
  61.6 0.0 copy-done.4
  61.6 0.3 fusion
  61.9 0.1 fusion.12
  62.0 0.6 broadcast.107.clone
  62.6 2.0 %scatter_fusion = f32[8,16,128]{2,1,0:T(8,128)} fusion(f32[8,16,128]{2,1,0:T(8,128)} %broadcast.107.clone, s32[4]{0:T(128)S(1)} %maximum_bitcast_fusion, f32[4,16,128]{2,1,0:T(8,128)S(1)} %fusion.12), kind=kCustom, calls=%fused_computation.3 | custom fusion | flops 8192 | bytes 98320 | tf_op jit(solution)/shard_map/scatter-add | solution.py:20
  64.6 0.0 copy-start.10
  64.6 3.6 %all-to-all-start = ((f32[8,16,128]{2,1,0:T(8,128)}), f32[8,16,128]{2,1,0:T(8,128)S(1)}, u32[]{:S(2)}, u32[]{:S(2)}) async-start(f32[8,16,128]{2,1,0:T(8,128)} %scatter_fusion), calls=%async_computation | async-start | bytes 131072 | tf_op jit(solution)/shard_map/all_to_all | solution.py:73
  68.1 0.0 copy-done.10
  68.2 0.1 broadcast_bitcast_fusion
  68.3 0.1 copy.42
  68.4 0.1 reshape.161
  68.5 5.6 %all-to-all-done = f32[8,16,128]{2,1,0:T(8,128)S(1)} async-done(((f32[8,16,128]{2,1,0:T(8,128)}), f32[8,16,128]{2,1,0:T(8,128)S(1)}, u32[]{:S(2)}, u32[]{:S(2)}) %all-to-all-start) | async-done | bytes 65568 | tf_op jit(solution)/shard_map/all_to_all | solution.py:73
  74.1 0.5 gather_fusion.1
  74.6 0.0 copy-start.7
  74.6 0.2 fusion.20
  74.8 0.1 copy.41
  74.9 39.3 %psum.29 = f32[16]{0:T(128)S(1)} all-reduce(f32[16]{0:T(128)S(1)} %fusion.20), channel_id=1, replica_groups=mesh['grp'=4,'sub'=8] {'grp','sub'}, use_global_device_ids=true, to_apply=%region_3.5 | all-reduce | flops 16 | bytes 128 | tf_op jit(solution)/shard_map/psum | solution.py:77
  114.2 0.0 copy-done.12
  114.2 0.0 copy-done.7
  114.2 0.1 convert_bitcast_fusion
  114.3 0.0 copy-start.2
  114.4 0.0 copy-done.3
  114.4 0.2 fusion.2
  114.5 0.1 fusion.11
  114.6 0.6 broadcast.107
  115.3 2.0 %scatter_fusion.1 = f32[8,16,128]{2,1,0:T(8,128)} fusion(f32[8,16,128]{2,1,0:T(8,128)} %broadcast.107, s32[4]{0:T(128)S(1)} %maximum_bitcast_fusion, f32[4,16,128]{2,1,0:T(8,128)S(1)} %fusion.11), kind=kCustom, calls=%fused_computation.4 | custom fusion | flops 8192 | bytes 98320 | tf_op jit(solution)/shard_map/scatter-add | solution.py:20
  117.2 3.3 %all-to-all-start.1 = ((f32[8,16,128]{2,1,0:T(8,128)}), f32[8,16,128]{2,1,0:T(8,128)S(1)}, u32[]{:S(2)}, u32[]{:S(2)}) async-start(f32[8,16,128]{2,1,0:T(8,128)} %scatter_fusion.1), calls=%async_computation.1 | async-start | bytes 131072 | tf_op jit(solution)/shard_map/all_to_all | solution.py:82
  120.6 0.6 gather_fusion
  121.2 0.0 copy-done
  121.2 0.3 convolution_bitcast_fusion
  121.5 4.9 %all-to-all-done.1 = f32[8,16,128]{2,1,0:T(8,128)S(1)} async-done(((f32[8,16,128]{2,1,0:T(8,128)}), f32[8,16,128]{2,1,0:T(8,128)S(1)}, u32[]{:S(2)}, u32[]{:S(2)}) %all-to-all-start.1) | async-done | bytes 65568 | tf_op jit(solution)/shard_map/all_to_all | solution.py:82
  126.4 0.5 gather_fusion.2
  127.0 0.2 multiply_reduce_fusion
  127.2 13.8 %psum.30 = f32[16]{0:T(128)S(1)} all-reduce(f32[16]{0:T(128)S(1)} %broadcast_multiply_fusion), channel_id=1, replica_groups=mesh['grp'=4,'sub'=8] {'sub'}, use_global_device_ids=true, to_apply=%region_6.8 | all-reduce | flops 16 | bytes 128 | tf_op jit(solution)/shard_map/psum | solution.py:93
  141.0 10.7 %psum.31 = f32[16]{0:T(128)S(1)} all-reduce(f32[16]{0:T(128)S(1)} %psum.30), channel_id=1, replica_groups=mesh['grp'=4,'sub'=8] {'grp'}, use_global_device_ids=true, to_apply=%region_7.9 | all-reduce | flops 16 | bytes 128 | tf_op jit(solution)/shard_map/psum | solution.py:93
  151.7 0.0 copy-done.13
  151.7 0.0 copy-done.2
  151.7 0.0 copy-done.6
  151.7 0.0 copy-start.5
  151.7 0.7 fusion.21
  152.4 0.1 copy-done.5
  152.5 0.7 add_convert_fusion
  (16 shorter events, 0.1 us)
Async XLA Ops:
  0.6 120.5 %copy-start = (bf16[1,1,12,2,128,128]{5,4,3,2,1,0:T(8,128)(2,1)S(1)}, bf16[1,1,12,2,128,128]{5,4,3,2,1,0:T(8,128)(2,1)}, u32[]{:S(2)}) copy-start(bf16[1,1,12,2,128,128]{5,4,3,2,1,0:T(8,128)(2,1)} %param.27) | copy-start | bytes 2359300
  0.6 0.7 copy-start.14
  1.4 0.7 copy-start.8
  3.0 0.7 copy-start.11
  3.7 42.2 %copy-start.9 = (f32[15,120]{1,0:T(8,128)S(1)}, f32[15,120]{1,0:T(8,128)}, u32[]{:S(2)}) copy-start(f32[15,120]{1,0:T(8,128)} %param.29) | copy-start | bytes 21604
  3.9 42.3 %copy-start.1 = (f32[1,1,16,512]{3,2,1,0:T(8,128)S(1)}, f32[1,1,16,512]{3,2,1,0:T(8,128)}, u32[]{:S(2)}) copy-start(f32[1,1,16,512]{3,2,1,0:T(8,128)} %param.17) | copy-start | bytes 98308
  47.3 14.3 %copy-start.4 = (f32[1,1,12,512]{3,1,2,0:T(1,128)S(1)}, f32[1,1,12,512]{3,1,2,0:T(1,128)}, u32[]{:S(2)}) copy-start(f32[1,1,12,512]{3,1,2,0:T(1,128)} %param.24) | copy-start | bytes 73732
  61.4 52.9 %copy-start.3 = (bf16[1,1,512,512]{3,2,1,0:T(8,128)(2,1)S(1)}, bf16[1,1,512,512]{3,2,1,0:T(8,128)(2,1)}, u32[]{:S(2)}) copy-start(bf16[1,1,512,512]{3,2,1,0:T(8,128)(2,1)} %param.26) | copy-start | bytes 1572868
  64.6 3.6 %copy-start.10 = (s32[1,1,12,2]{2,3,1,0:T(2,128)S(1)}, s32[1,1,12,2]{2,3,1,0:T(2,128)}, u32[]{:S(2)}) copy-start(s32[1,1,12,2]{2,3,1,0:T(2,128)} %param.28) | copy-start | bytes 292
  64.6 9.5 %all-to-all-start = ((f32[8,16,128]{2,1,0:T(8,128)}), f32[8,16,128]{2,1,0:T(8,128)S(1)}, u32[]{:S(2)}, u32[]{:S(2)}) async-start(f32[8,16,128]{2,1,0:T(8,128)} %scatter_fusion), calls=%async_computation | async-start | bytes 131072 | tf_op jit(solution)/shard_map/all_to_all | solution.py:73
  74.6 39.6 %copy-start.7 = (f32[1,1,16,512]{3,2,1,0:T(8,128)S(1)}, f32[1,1,16,512]{3,2,1,0:T(8,128)}, u32[]{:S(2)}) copy-start(f32[1,1,16,512]{3,2,1,0:T(8,128)} %param.18) | copy-start | bytes 98308
  74.9 39.3 %copy-start.12 = (f32[16]{0:T(128)S(1)}, f32[16]{0:T(128)}, u32[]{:S(2)}) copy-start(f32[16]{0:T(128)} %param.19) | copy-start | bytes 196
  114.2 37.5 %copy-start.13 = (f32[16]{0:T(128)}, f32[16]{0:T(128)S(1)}, u32[]{:S(2)}) copy-start(f32[16]{0:T(128)S(1)} %get-tuple-element.9) | copy-start | bytes 196
  114.3 37.4 %copy-start.2 = (f32[16,512]{1,0:T(8,128)}, f32[16,512]{1,0:T(8,128)S(1)}, u32[]{:S(2)}) copy-start(f32[16,512]{1,0:T(8,128)S(1)} %get-tuple-element.7) | copy-start | bytes 98308
  117.2 9.2 %all-to-all-start.1 = ((f32[8,16,128]{2,1,0:T(8,128)}), f32[8,16,128]{2,1,0:T(8,128)S(1)}, u32[]{:S(2)}, u32[]{:S(2)}) async-start(f32[8,16,128]{2,1,0:T(8,128)} %scatter_fusion.1), calls=%async_computation.1 | async-start | bytes 131072 | tf_op jit(solution)/shard_map/all_to_all | solution.py:82
  141.0 10.7 %copy-start.6 = (f32[1,1,16,512]{3,2,1,0:T(8,128)S(1)}, f32[1,1,16,512]{3,2,1,0:T(8,128)}, u32[]{:S(2)}) copy-start(f32[1,1,16,512]{3,2,1,0:T(8,128)} %param.16) | copy-start | bytes 98308
  151.7 0.8 copy-start.5
